TPU v7x, 32 devices: a whole 2x2x4 slice. The times are simulated.
32 devices in a mesh: groups: 2 (over y), tp: 16 (over z, x, core).
Axes of the slice: x: 2, y: 2, z: 4, core: 2. Of those that a mesh axis runs over, the one named last changes fastest.
Arguments:
- cached_block_pool: bfloat16 [2048, 8192], P(('groups', 'tp')), parts along dimension 0
- prefix_block_indices: int32 [256], P('groups'), parts along dimension 0, may hold values from 0 to 255, as said below
- trailing_new_rows: bfloat16 [512, 8192], P(('groups', 'tp')), parts along dimension 0
- input_norm_gain: bfloat16 [8192], replicated, may hold values from 0.099609375 to 1.8984375
- gate_projection_matrix: bfloat16 [28672, 8192], P('tp'), may hold values from -0.0625 to 0.0625
- up_projection_matrix: bfloat16 [28672, 8192], P('tp'), may hold values from -0.0625 to 0.0625
- down_projection_matrix: bfloat16 [28672, 8192], P('tp'), may hold values from -0.03125 to 0.03125
- gate_adapter_first: bfloat16 [8192, 16], replicated, may hold values from -0.0625 to 0.0625
- gate_adapter_second: bfloat16 [16, 28672], P(None, 'tp'), may hold values from -0.75 to 0.75
- up_adapter_first: bfloat16 [8192, 16], replicated, may hold values from -0.0625 to 0.0625
- up_adapter_second: bfloat16 [16, 28672], P(None, 'tp'), may hold values from -0.75 to 0.75
- down_adapter_first: bfloat16 [28672, 16], P('tp'), may hold values from -0.03125 to 0.03125
- down_adapter_second: bfloat16 [16, 8192], replicated, may hold values from -0.75 to 0.75
- output_cotangent_rows: bfloat16 [1536, 8192], P(('groups', 'tp')), parts along dimension 0, may hold values from -0.119628906 to 0.119628906
Outputs:
- gradient_gate_first: float32 [16384, 16], P(('groups', 'tp')), parts along dimension 0
- gradient_gate_second: float32 [16, 57344], P(None, ('groups', 'tp')), parts along dimension 1
- gradient_up_first: float32 [16384, 16], P(('groups', 'tp')), parts along dimension 0
- gradient_up_second: float32 [16, 57344], P(None, ('groups', 'tp')), parts along dimension 1
- gradient_down_first: float32 [57344, 16], P(('groups', 'tp')), parts along dimension 0
- gradient_down_second: float32 [16, 16384], P(None, ('groups', 'tp')), parts along dimension 1
There are 2 independent parts, one for each index of `groups`. A program takes and returns all parts, laid end to end along the dimension named above; an argument that names none is the same for every part. Nothing has to cross between parts.
Inputs may be any that keep to these rules, and one draw needn't show every extreme that they name: `prefix_block_indices`: at most 8 entries name blocks held by one device of tp, and the blocks of some device are named exactly 8 times; entries may repeat.
All inputs are finite; a program needn't handle non-finite values.
Results may differ from a plain program's by a relative error of at most 0.0069.
Values may be sent and summed in bfloat16 or wider, within the bound.
A program may use at most 256 MiB of HBM per device.

v0:
```python
import jax
import jax.numpy as jnp
from jax import lax
from jax.sharding import PartitionSpec as P

BLOCK = 4


ADAPTER_SCALE = 2.0


def narrow_product(left, right):
    return jnp.dot(
        left.astype(jnp.float32), right.astype(jnp.float32), precision=lax.Precision.HIGHEST
    )


def shards(
    cached_block_pool,
    prefix_block_indices,
    trailing_new_rows,
    input_norm_gain,
    gate_projection_matrix,
    up_projection_matrix,
    down_projection_matrix,
    gate_adapter_first,
    gate_adapter_second,
    up_adapter_first,
    up_adapter_second,
    down_adapter_first,
    down_adapter_second,
    output_cotangent_rows,
):
    devices = lax.axis_size("tp")
    my_index = lax.axis_index("tp")
    columns = cached_block_pool.shape[1]
    stored = cached_block_pool.reshape(-1, BLOCK, columns)
    block_count = prefix_block_indices.shape[0]
    owners = prefix_block_indices % devices
    places = prefix_block_indices // devices
    capacity = (block_count + devices - 1) // devices
    same_owner = owners[:, None] == owners[None, :]
    earlier = jnp.arange(block_count)[None, :] < jnp.arange(block_count)[:, None]
    ranking = jnp.sum(jnp.where(same_owner & earlier, 1, 0), axis=1).astype(jnp.int32)
    picked = (owners[None, :] == my_index) & (ranking[None, :] == jnp.arange(capacity)[:, None])
    local_slot = jnp.sum(jnp.where(picked, places[None, :], 0), axis=1)
    filled = jnp.any(picked, axis=1)
    packed = jnp.where(filled[:, None, None], stored[local_slot], jnp.zeros((), jnp.bfloat16))
    packed = packed.reshape(capacity * BLOCK, columns)
    wanted = owners * capacity + ranking
    arrived = lax.all_gather(packed, "tp", axis=0, tiled=True).reshape(
        devices * capacity, BLOCK, columns
    )
    prefix = arrived[wanted]
    prefix = prefix.reshape(block_count * BLOCK, columns)
    suffix_all, gradient_every_row = (
        lax.all_gather(trailing_new_rows, "tp", axis=0, tiled=True),
        lax.all_gather(output_cotangent_rows, "tp", axis=0, tiled=True),
    )
    rows = jnp.concatenate([prefix, suffix_all], axis=0)
    widened = rows.astype(jnp.float32)
    scale_rows = lax.rsqrt(jnp.mean(widened * widened, axis=1, keepdims=True) + 1e-05)
    normalized_rows = (widened * scale_rows * input_norm_gain.astype(jnp.float32)).astype(
        jnp.bfloat16
    )
    gate_rank_product = narrow_product(normalized_rows, gate_adapter_first).astype(jnp.bfloat16)
    up_rank_product = narrow_product(normalized_rows, up_adapter_first).astype(jnp.bfloat16)
    gate_projected_rows = jnp.dot(
        normalized_rows, gate_projection_matrix.T, preferred_element_type=jnp.float32
    ) + ADAPTER_SCALE * narrow_product(gate_rank_product, gate_adapter_second)
    up_projected_rows = jnp.dot(
        normalized_rows, up_projection_matrix.T, preferred_element_type=jnp.float32
    ) + ADAPTER_SCALE * narrow_product(up_rank_product, up_adapter_second)
    sigmoid_gate = jax.nn.sigmoid(gate_projected_rows)
    activated = gate_projected_rows * sigmoid_gate
    hidden_activation = (activated * up_projected_rows).astype(jnp.bfloat16)
    down_partial_sum = narrow_product(hidden_activation, down_adapter_first)
    gradient_rank_product = narrow_product(gradient_every_row, down_adapter_second.T).astype(
        jnp.bfloat16
    )
    gradient_hidden_units = jnp.dot(
        gradient_every_row, down_projection_matrix.T, preferred_element_type=jnp.float32
    ) + ADAPTER_SCALE * narrow_product(gradient_rank_product, down_adapter_first.T)
    gradient_gate_rows = (
        gradient_hidden_units
        * up_projected_rows
        * sigmoid_gate
        * (1.0 + gate_projected_rows * (1.0 - sigmoid_gate))
    ).astype(jnp.bfloat16)
    gradient_up_rows = (gradient_hidden_units * activated).astype(jnp.bfloat16)
    gate_partial_sum = narrow_product(gradient_gate_rows, gate_adapter_second.T)
    up_partial_sum = narrow_product(gradient_up_rows, up_adapter_second.T)
    gradient_gate_second = ADAPTER_SCALE * narrow_product(gate_rank_product.T, gradient_gate_rows)
    gradient_up_second = ADAPTER_SCALE * narrow_product(up_rank_product.T, gradient_up_rows)
    gradient_down_first = ADAPTER_SCALE * narrow_product(hidden_activation.T, gradient_rank_product)
    gate_gradient_term = ADAPTER_SCALE * narrow_product(normalized_rows.T, gate_partial_sum)
    up_gradient_term = ADAPTER_SCALE * narrow_product(normalized_rows.T, up_partial_sum)
    down_gradient_term = ADAPTER_SCALE * narrow_product(down_partial_sum.T, gradient_every_row)
    gradient_gate_first, gradient_up_first, gradient_down_second = (
        lax.psum_scatter(gate_gradient_term, "tp", scatter_dimension=0, tiled=True),
        lax.psum_scatter(up_gradient_term, "tp", scatter_dimension=0, tiled=True),
        lax.psum_scatter(down_gradient_term, "tp", scatter_dimension=1, tiled=True),
    )
    return (
        gradient_gate_first,
        gradient_gate_second,
        gradient_up_first,
        gradient_up_second,
        gradient_down_first,
        gradient_down_second,
    )


def solution(mesh):
    return jax.shard_map(
        shards,
        mesh=mesh,
        in_specs=(
            P(("groups", "tp"), None),
            P("groups"),
            P(("groups", "tp"), None),
            P(),
            P("tp", None),
            P("tp", None),
            P("tp", None),
            P(),
            P(None, "tp"),
            P(),
            P(None, "tp"),
            P("tp", None),
            P(),
            P(("groups", "tp"), None),
        ),
        out_specs=(
            P(("groups", "tp"), None),
            P(None, ("groups", "tp")),
            P(("groups", "tp"), None),
            P(None, ("groups", "tp")),
            P(("groups", "tp"), None),
            P(None, ("groups", "tp")),
        ),
        check_vma=False,
    )
```

profile of v0, /device:TPU:0, one launch (start us, length us, event | category | flops | bytes accessed | tf_op | source)
XLA Modules:
  0.0 477.5 jit_solution(15181177621398551961)
XLA Ops:
  9.2 1.5 reshape.53
  10.7 1.0 gather_fusion
  11.8 0.9 broadcast_select_fusion
  15.0 75.5 %all-gather.4.cloned.1.call-done = bf16[512,8192]{1,0:T(8,128)(2,1)} async-done(((bf16[32,8192]{1,0:T(8,128)(2,1)}), bf16[512,8192]{1,0:T(8,128)(2,1)}) %all-gather.4.cloned.1.call-update) | async-done | bytes 8388624 | tf_op jit(solution)/shard_map/all_gather | solution.py:51
  90.5 13.1 %reshape.54 = bf16[128,4,8192]{2,1,0:T(4,128)(2,1)} reshape(bf16[512,8192]{1,0:T(8,128)(2,1)} %all-gather.4.cloned.1.call-done) | data formatting | bytes 16777216 | tf_op jit(solution)/shard_map/reshape | solution.py:51
  103.6 14.1 %gather_fusion.1 = bf16[128,4,8192]{2,1,0:T(4,128)(2,1)} fusion(bf16[128,4,8192]{2,1,0:T(4,128)(2,1)} %reshape.54, s32[1024]{0:T(1024)S(1)} %pad_clamp_fusion), kind=kCustom, calls=%fused_computation.1 | custom fusion | bytes 16777728 | tf_op jit(solution)/shard_map/gather | solution.py:54
  117.7 12.5 %reshape.55 = bf16[512,8192]{1,0:T(8,128)(2,1)} reshape(bf16[128,4,8192]{2,1,0:T(4,128)(2,1)} %gather_fusion.1) | data formatting | bytes 16777216 | tf_op jit(solution)/shard_map/reshape | solution.py:55
  130.2 11.4 %all-gather.6.cloned.1.call-done = bf16[256,8192]{1,0:T(8,128)(2,1)} async-done(((bf16[16,8192]{1,0:T(8,128)(2,1)}), bf16[256,8192]{1,0:T(8,128)(2,1)}) %all-gather.6.cloned.1.call-update) | async-done | bytes 4194320 | tf_op jit(solution)/shard_map/all_gather | solution.py:57
  141.7 9.0 %fusion = f32[768]{0:T(1024)S(1)} fusion(bf16[256,8192]{1,0:T(8,128)(2,1)} %all-gather.6.cloned.1.call-done, bf16[512,8192]{1,0:T(8,128)(2,1)} %reshape.55), kind=kLoop, calls=%fused_computation.4 | loop fusion | flops 37747968 | bytes 12585984 | tf_op jit(solution)/shard_map/reduce_sum | solution.py:62
  150.7 8.0 %fusion.2 = bf16[768,8192]{1,0:T(8,128)(2,1)S(1)} fusion(f32[8192]{0:T(1024)S(1)} %convert_element_type.19, f32[768]{0:T(1024)S(1)} %add_rsqrt_fusion, bf16[256,8192]{1,0:T(8,128)(2,1)S(1)} %copy-done.7, bf16[512,8192]{1,0:T(8,128)(2,1)S(1)} %copy-done.3), kind=kLoop, calls=%fused_computation.6 | loop fusion | flops 44040192 | bytes 25201664 | tf_op jit(solution)/shard_map/convert_element_type | solution.py:63
  158.8 3.3 convolution_convert_fusion
  162.1 28.5 %fusion.10 = f32[768,1792]{1,0:T(8,128)} fusion(bf16[768,8192]{1,0:T(8,128)(2,1)S(1)} %fusion.2, bf16[1792,8192]{1,0:T(8,128)(2,1)} %param.18), kind=kOutput, calls=%fused_computation.47 | convolution fusion | flops 22548578304 | bytes 47448064 | tf_op jit(solution)/shard_map/dot_general | solution.py:68
  190.6 6.0 %multiply_add_fusion = f32[768,1792]{1,0:T(8,128)} fusion(f32[768,1792]{1,0:T(8,128)} %fusion.10, bf16[768,16]{0,1:T(8,128)(2,1)S(1)} %convolution_convert_fusion, bf16[16,1792]{1,0:T(8,128)(2,1)S(1)} %copy-done.11), kind=kOutput, calls=%fused_computation.16 | convolution fusion | flops 46792704 | bytes 11091968 | tf_op jit(solution)/shard_map/dot_general | solution.py:13
  196.6 3.3 convolution_convert_fusion.1
  199.9 27.4 %fusion.9 = f32[768,1792]{1,0:T(8,128)} fusion(bf16[768,8192]{1,0:T(8,128)(2,1)S(1)} %fusion.2, bf16[1792,8192]{1,0:T(8,128)(2,1)} %param.19), kind=kOutput, calls=%fused_computation.46 | convolution fusion | flops 22548578304 | bytes 47448064 | tf_op jit(solution)/shard_map/dot_general | solution.py:71
  227.3 15.9 %all-gather.8.cloned.1.call-done = bf16[768,8192]{1,0:T(8,128)(2,1)} async-done(((bf16[48,8192]{1,0:T(8,128)(2,1)}), bf16[768,8192]{1,0:T(8,128)(2,1)}) %all-gather.8.cloned.1.call-update) | async-done | bytes 12582928 | tf_op jit(solution)/shard_map/all_gather | solution.py:58
  243.2 8.1 %convolution_convert_fusion.2 = bf16[768,16]{0,1:T(8,128)(2,1)S(1)} fusion(bf16[768,8192]{1,0:T(8,128)(2,1)} %all-gather.8.cloned.1.call-done, bf16[16,8192]{1,0:T(8,128)(2,1)S(1)} %copy-done.9), kind=kOutput, calls=%fused_computation.24 | convolution fusion | flops 201338880 | bytes 12869632 | tf_op jit(solution)/shard_map/dot_general | solution.py:13
  251.4 27.5 %fusion.8 = f32[768,1792]{1,0:T(8,128)} fusion(bf16[768,8192]{1,0:T(8,128)(2,1)S(1)} %copy-done.4, bf16[1792,8192]{1,0:T(8,128)(2,1)} %param.20), kind=kOutput, calls=%fused_computation.45 | convolution fusion | flops 22548578304 | bytes 47448064 | tf_op jit(solution)/shard_map/dot_general | solution.py:81
  278.9 3.6 multiply_add_fusion.2
  283.1 6.8 %multiply_convert_fusion = (bf16[768,1792]{1,0:T(8,128)(2,1)S(1)}, bf16[768,1792]{1,0:T(8,128)(2,1)}, bf16[768,1792]{1,0:T(8,128)(2,1)}) fusion(f32[768,1792]{1,0:T(8,128)} %multiply_add_fusion, f32[768,1792]{1,0:T(8,128)S(1)} %multiply_add_fusion.2, f32[768,1792]{1,0:T(8,128)S(1)} %copy-done.13, bf16[768,16]{0,1:T(8,128)(2,1)S(1)} %convolution_convert_fusion.1, ...), kind=kOutput, calls=%fused_computation.11 | convolution fusion | flops 67436544 | bytes 24854528 | tf_op jit(solution)/shard_map/dot_general | solution.py:13
  289.9 1.5 copy-done.6
  292.2 5.8 %convolution_multiply_fusion = f32[16,8192]{1,0:T(8,128)} fusion(f32[768,16]{0,1:T(8,128)S(1)} %fusion.13, bf16[768,8192]{1,0:T(8,128)(2,1)S(1)} %copy-done.4), kind=kOutput, calls=%fused_computation.8 | convolution fusion | flops 1208090624 | bytes 13156352 | tf_op jit(solution)/shard_map/dot_general | solution.py:13
  298.1 2.6 fusion.11
  300.7 2.7 fusion.12
  303.4 9.0 %convolution_multiply_fusion.2 = f32[8192,16]{0,1:T(8,128)} fusion(bf16[768,8192]{1,0:T(8,128)(2,1)} %copy-done.2, f32[768,16]{0,1:T(8,128)S(1)} %fusion.11), kind=kOutput, calls=%fused_computation.10 | convolution fusion | flops 1208090624 | bytes 13156352 | tf_op jit(solution)/shard_map/dot_general | solution.py:13
  312.5 8.9 %convolution_multiply_fusion.1 = f32[8192,16]{0,1:T(8,128)} fusion(bf16[768,8192]{1,0:T(8,128)(2,1)} %copy-done.2, f32[768,16]{0,1:T(8,128)S(1)} %fusion.12), kind=kOutput, calls=%fused_computation.9 | convolution fusion | flops 1208090624 | bytes 13156352 | tf_op jit(solution)/shard_map/dot_general | solution.py:13
  321.4 2.9 convolution_multiply_fusion.3
  324.3 2.9 convolution_multiply_fusion.5
  327.2 1.1 convolution_multiply_fusion.4
  328.4 23.8 %reduce-scatter.8.cloned.1.call-done = f32[16,512]{1,0:T(8,128)} async-done(((f32[16,8192]{1,0:T(8,128)}), f32[16,512]{1,0:T(8,128)}) %reduce-scatter.8.cloned.1.call-update) | async-done | bytes 32784 | tf_op jit(solution)/shard_map/reduce_scatter | solution.py:102
  352.2 59.2 %reduce-scatter.4.cloned.1.call-done = f32[512,16]{0,1:T(8,128)} async-done(((f32[8192,16]{0,1:T(8,128)}), f32[512,16]{0,1:T(8,128)}) %reduce-scatter.4.cloned.1.call-update) | async-done | bytes 32784 | tf_op jit(solution)/shard_map/reduce_scatter | solution.py:100
  411.4 58.8 %reduce-scatter.6.cloned.1.call-done = f32[512,16]{0,1:T(8,128)} async-done(((f32[8192,16]{0,1:T(8,128)}), f32[512,16]{0,1:T(8,128)}) %reduce-scatter.6.cloned.1.call-update) | async-done | bytes 32784 | tf_op jit(solution)/shard_map/reduce_scatter | solution.py:101
  (54 shorter events, 6.0 us)
Async XLA Ops:
  7.2 151.6 %copy-start = (bf16[8192,16]{0,1:T(8,128)(2,1)S(1)}, bf16[8192,16]{0,1:T(8,128)(2,1)}, u32[]{:S(2)}) copy-start(bf16[8192,16]{0,1:T(8,128)(2,1)} %param.21) | copy-start | bytes 786436
  7.2 83.3 %all-gather.4.cloned.1.call-start = ((), (), s32[]{:S(2)}) async-start(), calls=%async_computation.3 | async-start | bytes 8912896 | tf_op jit(solution)/shard_map/all_gather | solution.py:51
  12.8 128.9 %all-gather.6.cloned.1.call-start = ((), (), s32[]{:S(2)}) async-start(), calls=%async_computation.4 | async-start | bytes 4456448 | tf_op jit(solution)/shard_map/all_gather | solution.py:57
  13.5 229.7 %all-gather.8.cloned.1.call-start = ((), (), s32[]{:S(2)}) async-start(), calls=%async_computation.5 | async-start | bytes 13369344 | tf_op jit(solution)/shard_map/all_gather | solution.py:58
  14.2 337.9 %reduce-scatter.8.cloned.1.call-start = ((), (), s32[]{:S(2)}) async-start(), calls=%async_computation.8 | async-start | bytes 557056 | tf_op jit(solution)/shard_map/reduce_scatter | solution.py:102
  141.7 9.1 %copy-start.3 = (bf16[512,8192]{1,0:T(8,128)(2,1)S(1)}, bf16[512,8192]{1,0:T(8,128)(2,1)}, u32[]{:S(2)}) copy-start(bf16[512,8192]{1,0:T(8,128)(2,1)} %reshape.55) | copy-start | bytes 25165828
  141.7 9.1 %copy-start.7 = (bf16[256,8192]{1,0:T(8,128)(2,1)S(1)}, bf16[256,8192]{1,0:T(8,128)(2,1)}, u32[]{:S(2)}) copy-start(bf16[256,8192]{1,0:T(8,128)(2,1)} %all-gather.6.cloned.1.call-done) | copy-start | bytes 12582916
  158.8 41.2 %copy-start.2 = (bf16[768,8192]{1,0:T(8,128)(2,1)}, bf16[768,8192]{1,0:T(8,128)(2,1)S(1)}, u32[]{:S(2)}) copy-start(bf16[768,8192]{1,0:T(8,128)(2,1)S(1)} %fusion.2) | copy-start | bytes 37748740
  162.1 28.5 %copy-start.11 = (bf16[16,1792]{1,0:T(8,128)(2,1)S(1)}, bf16[16,1792]{1,0:T(8,128)(2,1)}, u32[]{:S(2)}) copy-start(bf16[16,1792]{1,0:T(8,128)(2,1)} %param.22) | copy-start | bytes 172036
  190.6 6.0 %copy-start.8 = (bf16[8192,16]{0,1:T(8,128)(2,1)S(1)}, bf16[8192,16]{0,1:T(8,128)(2,1)}, u32[]{:S(2)}) copy-start(bf16[8192,16]{0,1:T(8,128)(2,1)} %param.23) | copy-start | bytes 786436
  199.9 43.3 %copy-start.9 = (bf16[16,8192]{1,0:T(8,128)(2,1)S(1)}, bf16[16,8192]{1,0:T(8,128)(2,1)}, u32[]{:S(2)}) copy-start(bf16[16,8192]{1,0:T(8,128)(2,1)} %param.26) | copy-start | bytes 786436
  243.2 8.2 %copy-start.4 = (bf16[768,8192]{1,0:T(8,128)(2,1)S(1)}, bf16[768,8192]{1,0:T(8,128)(2,1)}, u32[]{:S(2)}) copy-start(bf16[768,8192]{1,0:T(8,128)(2,1)} %all-gather.8.cloned.1.call-done) | copy-start | bytes 37748740
  251.4 27.5 %copy-start.10 = (bf16[1792,16]{0,1:T(8,128)(2,1)S(1)}, bf16[1792,16]{0,1:T(8,128)(2,1)}, u32[]{:S(2)}) copy-start(bf16[1792,16]{0,1:T(8,128)(2,1)} %param.25) | copy-start | bytes 172036
  278.9 3.6 copy-start.12
  278.9 4.2 copy-start.13
  289.9 1.5 copy-start.6
  298.1 113.3 %reduce-scatter.4.cloned.1.call-start = ((), (), s32[]{:S(2)}) async-start(), calls=%async_computation.6 | async-start | bytes 557056 | tf_op jit(solution)/shard_map/reduce_scatter | solution.py:100
  312.4 14.8 %copy-start.5 = (bf16[768,1792]{1,0:T(8,128)(2,1)S(1)}, bf16[768,1792]{1,0:T(8,128)(2,1)}, u32[]{:S(2)}) copy-start(bf16[768,1792]{1,0:T(8,128)(2,1)} %get-tuple-element.10) | copy-start | bytes 8257540
  312.4 157.7 %copy-start.1 = (bf16[8192,16]{0,1:T(8,128)(2,1)S(1)}, bf16[8192,16]{0,1:T(8,128)(2,1)}, u32[]{:S(2)}) copy-start(bf16[8192,16]{0,1:T(8,128)(2,1)} %param.21) | copy-start | bytes 786436
  312.4 157.7 %reduce-scatter.6.cloned.1.call-start = ((), (), s32[]{:S(2)}) async-start(), calls=%async_computation.7 | async-start | bytes 557056 | tf_op jit(solution)/shard_map/reduce_scatter | solution.py:101
Sparse Core Ops, SparseCore 0:
  12.9 77.5 all-gather.3
  92.7 48.9 all-gather.5
  143.9 99.2 all-gather.7
  298.2 53.9 reduce-scatter.7
  356.5 54.7 reduce-scatter.3
  415.3 54.7 reduce-scatter.5
where the time goes:
time: 487 us; the launch traced here: 477 us
  waiting for transfers between devices  246 us (51%)
  matrix products  151 us (31%)
  local copies, waits for them, and re-layouts  44.7 us (9%)
  other arithmetic  20.5 us (4%)
  between operations  14.7 us (3%)
    all_gather x1, waiting for transfers between devices, shards(): lax.all_gather(packed, 'tp', axis=0, tiled=True)  75.5 us
    dot_general x15, matrix products, narrow_product(): jnp.dot(left.astype(jnp.float32), right.astype(jnp.float32), precision=la...  67.9 us
    reduce_scatter x1, waiting for transfers between devices, shards(): lax.psum_scatter(gate_gradient_term, 'tp', scatter_dimension=0, tiled=True)  59.2 us
    reduce_scatter x1, waiting for transfers between devices, shards(): lax.psum_scatter(up_gradient_term, 'tp', scatter_dimension=0, tiled=True)  58.8 us
    dot_general x1, matrix products, shards(): jnp.dot(normalized_rows, gate_projection_matrix.T, preferred_element_type...  28.5 us
    dot_general x1, matrix products, shards(): jnp.dot(gradient_every_row, down_projection_matrix.T, preferred_element_t...  27.5 us
    dot_general x1, matrix products, shards(): jnp.dot(normalized_rows, up_projection_matrix.T, preferred_element_type=j...  27.4 us
    reduce_scatter x1, waiting for transfers between devices, shards(): lax.psum_scatter(down_gradient_term, 'tp', scatter_dimension=1, tiled=True)  23.8 us
  transfers between devices with their start and end apart: 6, of which 6 were waited for; matrix products, arithmetic and copies ran while one was open for 33% of the time, Pallas kernels for 0%

commit v1 on v0

v1 whole, which is shorter than its diff:
```python
import jax
import jax.numpy as jnp
from jax import lax
from jax.sharding import PartitionSpec as P

BLOCK = 4
ADAPTER_SCALE = 2.0


def narrow(left, right, left_dim, right_dim):
    return lax.dot_general(
        left, right, (((left_dim,), (right_dim,)), ((), ())), preferred_element_type=jnp.float32
    )


def exact(left, right, left_dim, right_dim):
    return lax.dot_general(
        left.astype(jnp.float32),
        right.astype(jnp.float32),
        (((left_dim,), (right_dim,)), ((), ())),
        precision=lax.Precision.HIGHEST,
    )


def own_rows(pool, indices, suffix, gain, devices, my_index):
    count = indices.shape[0]
    capacity = count // devices
    owners = indices % devices
    places = indices // devices
    position = jnp.arange(count)
    before = (owners[:, None] == owners[None, :]) & (position[None, :] < position[:, None])
    ranking = jnp.sum(before.astype(jnp.int32), axis=1)
    picked = (owners[None, :] == my_index) & (ranking[None, :] == jnp.arange(capacity)[:, None])
    slot = jnp.sum(jnp.where(picked, places[None, :], 0), axis=1)
    source = (slot[:, None] * BLOCK + jnp.arange(BLOCK)[None, :]).reshape(-1)
    select = (source[:, None] == jnp.arange(pool.shape[0])[None, :]).astype(jnp.bfloat16)
    packed = narrow(select, pool, 1, 0)
    rows = jnp.concatenate([packed, suffix.astype(jnp.float32)], axis=0)
    scale = lax.rsqrt(jnp.mean(rows * rows, axis=1, keepdims=True) + 1e-05)
    normed = (rows * scale * gain.astype(jnp.float32)).astype(jnp.bfloat16)
    held, new = capacity * BLOCK, suffix.shape[0]
    per = held + new
    prefix_at = owners * per + ranking * BLOCK
    prefix_at = (prefix_at[:, None] + jnp.arange(BLOCK)[None, :]).reshape(-1)
    suffix_at = (jnp.arange(devices)[:, None] * per + held + jnp.arange(new)[None, :]).reshape(-1)
    arrived_at = jnp.concatenate([prefix_at, suffix_at])
    order = (arrived_at[:, None] == jnp.arange(devices * per)[None, :]).astype(jnp.bfloat16)
    return normed, order


def shards(
    cached_block_pool,
    prefix_block_indices,
    trailing_new_rows,
    input_norm_gain,
    gate_projection_matrix,
    up_projection_matrix,
    down_projection_matrix,
    gate_adapter_first,
    gate_adapter_second,
    up_adapter_first,
    up_adapter_second,
    down_adapter_first,
    down_adapter_second,
    output_cotangent_rows,
):
    devices = lax.axis_size("tp")
    my_index = lax.axis_index("tp")
    width = cached_block_pool.shape[1]
    rank = gate_adapter_first.shape[1]
    normed_own, order = own_rows(
        cached_block_pool,
        prefix_block_indices,
        trailing_new_rows,
        input_norm_gain,
        devices,
        my_index,
    )
    arrived = lax.all_gather(normed_own, "tp", axis=0, tiled=True)
    cotangent = lax.all_gather(output_cotangent_rows, "tp", axis=0, tiled=True)
    normed = narrow(order, arrived, 1, 0).astype(jnp.bfloat16)
    both_first = jnp.concatenate([gate_adapter_first, up_adapter_first], axis=1)
    low = narrow(normed, both_first, 1, 0).astype(jnp.bfloat16)
    gate_low, up_low = low[:, :rank], low[:, rank:]
    gate_proj = narrow(normed, gate_projection_matrix, 1, 1) + ADAPTER_SCALE * narrow(
        gate_low, gate_adapter_second, 1, 0
    )
    up_proj = narrow(normed, up_projection_matrix, 1, 1) + ADAPTER_SCALE * narrow(
        up_low, up_adapter_second, 1, 0
    )
    sigmoid = jax.nn.sigmoid(gate_proj)
    activated = gate_proj * sigmoid
    hidden = (activated * up_proj).astype(jnp.bfloat16)
    grad_low = narrow(cotangent, down_adapter_second, 1, 1).astype(jnp.bfloat16)
    grad_hidden = narrow(cotangent, down_projection_matrix, 1, 1) + ADAPTER_SCALE * narrow(
        grad_low, down_adapter_first, 1, 1
    )
    grad_gate = (
        grad_hidden * up_proj * sigmoid * (1.0 + gate_proj * (1.0 - sigmoid))
    ).astype(jnp.bfloat16)
    grad_up = (grad_hidden * activated).astype(jnp.bfloat16)
    partial = jnp.concatenate(
        [
            narrow(hidden, down_adapter_first, 1, 0),
            narrow(grad_gate, gate_adapter_second, 1, 1),
            narrow(grad_up, up_adapter_second, 1, 1),
        ],
        axis=1,
    )
    total = lax.psum(partial, "tp")
    gate_second = ADAPTER_SCALE * narrow(gate_low, grad_gate, 0, 0)
    up_second = ADAPTER_SCALE * narrow(up_low, grad_up, 0, 0)
    down_first = ADAPTER_SCALE * narrow(hidden, grad_low, 0, 0)
    mine = width // devices
    normed_mine = lax.dynamic_slice_in_dim(normed, my_index * mine, mine, 1)
    cotangent_mine = lax.dynamic_slice_in_dim(cotangent, my_index * mine, mine, 1)
    both = ADAPTER_SCALE * exact(normed_mine, total[:, rank:], 0, 0)
    down_second = ADAPTER_SCALE * exact(total[:, :rank], cotangent_mine, 0, 0)
    return both[:, :rank], gate_second, both[:, rank:], up_second, down_first, down_second


def solution(mesh):
    return jax.shard_map(
        shards,
        mesh=mesh,
        in_specs=(
            P(("groups", "tp"), None),
            P("groups"),
            P(("groups", "tp"), None),
            P(),
            P("tp", None),
            P("tp", None),
            P("tp", None),
            P(),
            P(None, "tp"),
            P(),
            P(None, "tp"),
            P("tp", None),
            P(),
            P(("groups", "tp"), None),
        ),
        out_specs=(
            P(("groups", "tp"), None),
            P(None, ("groups", "tp")),
            P(("groups", "tp"), None),
            P(None, ("groups", "tp")),
            P(("groups", "tp"), None),
            P(None, ("groups", "tp")),
        ),
        check_vma=False,
    )
```

time: 487 us -> 366 us (0.75); the launches traced: 477 us -> 365 us
  local copies, waits for them, and re-layouts: 44.7 us -> 1.63 us
  waiting for transfers between devices: 246 us -> 207 us
  other arithmetic: 20.5 us -> 5.77 us
  matrix products: 151 us -> 137 us
    reduce_scatter x3 -> x0, waiting for transfers between devices: 142 us -> none  [the longest x1 59.2 us: shards(): lax.psum_scatter(gate_gradient_term, 'tp', scatter_dimension=0, tiled=True)]
    psum x0 -> x1, waiting for transfers between devices: none -> 83.2 us  [shards(): total = lax.psum(partial, 'tp')]
    reshape x3 -> x0, local copies, waits for them, and re-layouts: 27.1 us -> none  [the longest x1 13.1 us: shards(): lax.all_gather(packed, 'tp', axis=0, tiled=True)]
    all_gather x3 -> x2, waiting for transfers between devices: 103 us -> 123 us  [the longest x1 102 us: shards(): arrived = lax.all_gather(normed_own, 'tp', axis=0, tiled=True)]
    gather x3 -> x0, local copies, waits for them, and re-layouts: 15.2 us -> none  [the longest x1 14.1 us: shards(): prefix = arrived[wanted]]
    dot_general x18, matrix products: 151 us -> 137 us  [the longest x16 133 us: narrow(): lax.dot_general(left, right, (((left_dim,), (right_dim,)), ((), ())), pre...]
    reduce_sum x3, other arithmetic: 9.32 us -> 0.53 us  [the longest x1 0.24 us: own_rows(): scale = lax.rsqrt(jnp.mean(rows * rows, axis=1, keepdims=True) + 1e-05)]
    convert_element_type x2 -> x3, other arithmetic: 8.75 us -> 2.88 us  [the longest x2 1.9 us: own_rows(): normed = (rows * scale * gain.astype(jnp.float32)).astype(jnp.bfloat16)]
  transfers between devices with their start and end apart: 6 -> 3, of which waited for: 6 -> 3; matrix products, arithmetic and copies ran while one was open for 33% -> 23% of each run, Pallas kernels for 0% -> 0%
where the time goes in v1:
time: 366 us; the launch traced here: 365 us
  waiting for transfers between devices  207 us (57%)
  matrix products  137 us (37%)
  between operations  13.9 us (4%)
  other arithmetic  5.77 us (2%)
    dot_general x16, matrix products, narrow(): lax.dot_general(left, right, (((left_dim,), (right_dim,)), ((), ())), pre...  133 us
    all_gather x1, waiting for transfers between devices, shards(): arrived = lax.all_gather(normed_own, 'tp', axis=0, tiled=True)  102 us
    psum x1, waiting for transfers between devices, shards(): total = lax.psum(partial, 'tp')  83.2 us
    all_gather x1, waiting for transfers between devices, shards(): cotangent = lax.all_gather(output_cotangent_rows, 'tp', axis=0, tiled=True)  20.9 us
  transfers between devices with their start and end apart: 3, of which 3 were waited for; matrix products, arithmetic and copies ran while one was open for 23% of the time, Pallas kernels for 0%

profile of v1, /device:TPU:0, one launch (start us, length us, event | category | flops | bytes accessed | tf_op | source)
XLA Modules:
  0.0 365.4 jit_solution(2630337641439258280)
XLA Ops:
  7.2 0.7 and_select_fusion
  8.0 0.7 broadcast_compare_fusion
  8.6 0.2 convert_reduce_fusion
  9.1 0.7 convert_element_type.36
  9.8 1.0 convert_element_type.35
  10.8 0.3 fusion.14
  11.2 0.2 multiply_reduce_fusion
  11.4 1.2 multiply_convert_fusion.3
  12.7 0.7 all-gather.5.cloned.1.call-update
  13.8 102.4 %all-gather.3.cloned.1.call-done = bf16[768,8192]{1,0:T(8,128)(2,1)} async-done(((bf16[48,8192]{1,0:T(8,128)(2,1)}), bf16[768,8192]{1,0:T(8,128)(2,1)}) %all-gather.3.cloned.1.call-update) | async-done | bytes 12582928 | tf_op jit(solution)/shard_map/all_gather | solution.py:79
  116.2 15.2 %convolution_convert_fusion = bf16[768,8192]{1,0:T(8,128)(2,1)S(1)} fusion(bf16[768,8192]{1,0:T(8,128)(2,1)} %all-gather.3.cloned.1.call-done, s32[768]{0:T(1024)S(1)} %pad_add_fusion), kind=kOutput, calls=%fused_computation | convolution fusion | flops 9670557696 | bytes 25168896 | tf_op jit(solution)/shard_map/dot_general | solution.py:11
  131.5 3.8 %convolution_convert_fusion.1 = bf16[768,32]{0,1:T(8,128)(2,1)S(1)} fusion(bf16[768,8192]{1,0:T(8,128)(2,1)S(1)} %convolution_convert_fusion, bf16[8192,16]{0,1:T(8,128)(2,1)S(1)} %copy-done.5, bf16[8192,16]{0,1:T(8,128)(2,1)S(1)} %copy-done.6), kind=kOutput, calls=%fused_computation.17 | convolution fusion | flops 403726336 | bytes 13156352 | tf_op jit(solution)/shard_map/dot_general | solution.py:11
  135.3 27.8 %fusion.21 = f32[768,1792]{1,0:T(8,128)} fusion(bf16[768,8192]{1,0:T(8,128)(2,1)S(1)} %convolution_convert_fusion, bf16[1792,8192]{1,0:T(8,128)(2,1)} %param.18), kind=kOutput, calls=%fused_computation.60 | convolution fusion | flops 22548578304 | bytes 47448064 | tf_op jit(solution)/shard_map/dot_general | solution.py:11
  163.1 5.9 %multiply_add_fusion.2 = f32[768,1792]{1,0:T(8,128)} fusion(f32[768,1792]{1,0:T(8,128)} %fusion.21, bf16[16,1792]{1,0:T(8,128)(2,1)S(1)} %copy-done.9, bf16[768,32]{0,1:T(8,128)(2,1)S(1)} %convolution_convert_fusion.1), kind=kOutput, calls=%fused_computation.8 | convolution fusion | flops 46792704 | bytes 11091968 | tf_op jit(solution)/shard_map/dot_general | solution.py:11
  169.0 27.6 %fusion.22 = f32[768,1792]{1,0:T(8,128)} fusion(bf16[768,8192]{1,0:T(8,128)(2,1)S(1)} %convolution_convert_fusion, bf16[1792,8192]{1,0:T(8,128)(2,1)} %param.19), kind=kOutput, calls=%fused_computation.61 | convolution fusion | flops 22548578304 | bytes 47448064 | tf_op jit(solution)/shard_map/dot_general | solution.py:11
  196.6 20.9 %all-gather.5.cloned.1.call-done = bf16[768,8192]{1,0:T(8,128)(2,1)} async-done(((bf16[48,8192]{1,0:T(8,128)(2,1)}), bf16[768,8192]{1,0:T(8,128)(2,1)}) %all-gather.5.cloned.1.call-update) | async-done | bytes 12582928 | tf_op jit(solution)/shard_map/all_gather | solution.py:80
  217.5 8.1 %convolution_convert_fusion.2 = bf16[768,16]{0,1:T(8,128)(2,1)S(1)} fusion(bf16[768,8192]{1,0:T(8,128)(2,1)} %all-gather.5.cloned.1.call-done, bf16[16,8192]{1,0:T(8,128)(2,1)S(1)} %copy-done.7), kind=kOutput, calls=%fused_computation.19 | convolution fusion | flops 201338880 | bytes 12869632 | tf_op jit(solution)/shard_map/dot_general | solution.py:11
  225.6 27.3 %fusion.24 = f32[768,1792]{1,0:T(8,128)} fusion(bf16[768,8192]{1,0:T(8,128)(2,1)S(1)} %copy-done.4, bf16[1792,8192]{1,0:T(8,128)(2,1)} %param.20), kind=kOutput, calls=%fused_computation.63 | convolution fusion | flops 22548578304 | bytes 47448064 | tf_op jit(solution)/shard_map/dot_general | solution.py:11
  253.0 3.6 multiply_add_fusion
  256.6 0.6 copy-done.11
  257.2 5.5 %multiply_convert_fusion.2 = (bf16[768,1792]{1,0:T(8,128)(2,1)S(1)}, bf16[768,1792]{1,0:T(8,128)(2,1)S(1)}, bf16[768,1792]{1,0:T(8,128)(2,1)S(1)}) fusion(f32[768,1792]{1,0:T(8,128)} %multiply_add_fusion.2, f32[768,1792]{1,0:T(8,128)S(1)} %multiply_add_fusion, f32[768,1792]{1,0:T(8,128)S(1)} %copy-done.11, bf16[16,1792]{1,0:T(8,128)(2,1)S(1)} %copy-done.10, ...), kind=kOutput, calls=%fused_computation.4 | convolution fusion | flops 67436544 | bytes 24854528 | tf_op jit(solution)/shard_map/dot_general | solution.py:11
  262.8 0.8 fusion.23
  263.6 1.2 convolution_multiply_fusion
  264.8 0.8 fusion.25
  265.6 1.2 convolution_multiply_fusion.2
  266.8 0.8 fusion.26
  267.6 0.7 pad_maximum_fusion.1
  268.3 2.9 convolution_multiply_fusion.1
  271.2 83.2 %all-reduce.2.cloned.1.call-done = f32[768,48]{0,1:T(8,128)} async-done(((f32[768,48]{0,1:T(8,128)}), f32[768,48]{0,1:T(8,128)}) %all-reduce.2.cloned.1.call-update) | async-done | bytes 147472 | tf_op jit(solution)/shard_map/psum | solution.py:110
  354.4 1.6 convolution_multiply_fusion.3
  356.0 0.6 fusion.20
  356.7 2.2 convolution_multiply_fusion.4
  (40 shorter events, 0.9 us)
Async XLA Ops:
  7.2 3.7 %copy-start = (bf16[64,8192]{1,0:T(8,128)(2,1)S(1)}, bf16[64,8192]{1,0:T(8,128)(2,1)}, u32[]{:S(2)}) copy-start(bf16[64,8192]{1,0:T(8,128)(2,1)} %param.14) | copy-start | bytes 3145732
  7.2 109.1 %all-gather.3.cloned.1.call-start = ((), (), s32[]{:S(2)}) async-start(), calls=%async_computation | async-start | bytes 13369344 | tf_op jit(solution)/shard_map/all_gather | solution.py:79
  12.6 204.9 %all-gather.5.cloned.1.call-start = ((), (), s32[]{:S(2)}) async-start(), calls=%async_computation.1 | async-start | bytes 13369344 | tf_op jit(solution)/shard_map/all_gather | solution.py:80
  13.4 341.0 %all-reduce.2.cloned.1.call-start = ((), (), s32[]{:S(2)}) async-start(), calls=%async_computation.2 | async-start | bytes 294912 | tf_op jit(solution)/shard_map/psum | solution.py:110
  13.8 117.7 %copy-start.5 = (bf16[8192,16]{0,1:T(8,128)(2,1)S(1)}, bf16[8192,16]{0,1:T(8,128)(2,1)}, u32[]{:S(2)}) copy-start(bf16[8192,16]{0,1:T(8,128)(2,1)} %param.23) | copy-start | bytes 786436
  13.8 117.7 %copy-start.6 = (bf16[8192,16]{0,1:T(8,128)(2,1)S(1)}, bf16[8192,16]{0,1:T(8,128)(2,1)}, u32[]{:S(2)}) copy-start(bf16[8192,16]{0,1:T(8,128)(2,1)} %param.21) | copy-start | bytes 786436
  131.5 37.5 %copy-start.3 = (bf16[768,8192]{1,0:T(8,128)(2,1)}, bf16[768,8192]{1,0:T(8,128)(2,1)S(1)}, u32[]{:S(2)}) copy-start(bf16[768,8192]{1,0:T(8,128)(2,1)S(1)} %convolution_convert_fusion) | copy-start | bytes 37748740
  135.3 27.8 %copy-start.9 = (bf16[16,1792]{1,0:T(8,128)(2,1)S(1)}, bf16[16,1792]{1,0:T(8,128)(2,1)}, u32[]{:S(2)}) copy-start(bf16[16,1792]{1,0:T(8,128)(2,1)} %param.22) | copy-start | bytes 172036
  169.0 48.5 %copy-start.7 = (bf16[16,8192]{1,0:T(8,128)(2,1)S(1)}, bf16[16,8192]{1,0:T(8,128)(2,1)}, u32[]{:S(2)}) copy-start(bf16[16,8192]{1,0:T(8,128)(2,1)} %param.26) | copy-start | bytes 786436
  217.5 8.2 %copy-start.4 = (bf16[768,8192]{1,0:T(8,128)(2,1)S(1)}, bf16[768,8192]{1,0:T(8,128)(2,1)}, u32[]{:S(2)}) copy-start(bf16[768,8192]{1,0:T(8,128)(2,1)} %all-gather.5.cloned.1.call-done) | copy-start | bytes 37748740
  225.6 27.3 %copy-start.8 = (bf16[1792,16]{0,1:T(8,128)(2,1)S(1)}, bf16[1792,16]{0,1:T(8,128)(2,1)}, u32[]{:S(2)}) copy-start(bf16[1792,16]{0,1:T(8,128)(2,1)} %param.25) | copy-start | bytes 172036
  253.0 3.6 copy-start.10
  253.0 4.2 %copy-start.11 = (f32[768,1792]{1,0:T(8,128)S(1)}, f32[768,1792]{1,0:T(8,128)}, u32[]{:S(2)}) copy-start(f32[768,1792]{1,0:T(8,128)} %fusion.22) | copy-start | bytes 16515076
  262.8 4.0 %copy-start.2 = (bf16[768,1792]{1,0:T(8,128)(2,1)}, bf16[768,1792]{1,0:T(8,128)(2,1)S(1)}, u32[]{:S(2)}) copy-start(bf16[768,1792]{1,0:T(8,128)(2,1)S(1)} %get-tuple-element.10) | copy-start | bytes 8257540
  265.6 93.3 %copy-start.1 = (bf16[64,8192]{1,0:T(8,128)(2,1)S(1)}, bf16[64,8192]{1,0:T(8,128)(2,1)}, u32[]{:S(2)}) copy-start(bf16[64,8192]{1,0:T(8,128)(2,1)} %param.14) | copy-start | bytes 3145732
Sparse Core Ops, SparseCore 0:
  12.7 103.4 all-gather.2
  118.5 98.9 all-gather.4
  268.4 85.9 all-reduce.1

commit v2 on v1

--- a/solution.py
+++ b/solution.py
@@ -1,6 +1,8 @@
 import jax
 import jax.numpy as jnp
 from jax import lax
+from jax.experimental import pallas as pl
+from jax.experimental.pallas import tpu as pltpu
 from jax.sharding import PartitionSpec as P
 
 BLOCK = 4
@@ -46,6 +48,433 @@
     arrived_at = jnp.concatenate([prefix_at, suffix_at])
     order = (arrived_at[:, None] == jnp.arange(devices * per)[None, :]).astype(jnp.bfloat16)
     return normed, order
+
+
+MESH = pl.DeviceIdType.MESH
+TILE = 256
+PANEL = 640
+CHUNK = 2048
+STRIP = 128
+
+
+def layer_kernel(
+    rows_own,
+    cotangent_own,
+    order,
+    gate_w,
+    up_w,
+    down_w,
+    gate_ext,
+    down_ext,
+    hidden_back,
+    gate_back,
+    up_back,
+    arrived,
+    summed_out,
+    gate_second,
+    up_second,
+    down_first,
+    rows_mine,
+    cotangent_mine,
+    rows,
+    cotangent,
+    weights,
+    projected,
+    panels,
+    total,
+    hidden,
+    grad_gate,
+    grad_up,
+    weight_sem,
+    panel_sem,
+    own_sem,
+    send_sem,
+    recv_sem,
+    partial,
+    pieces,
+    summed,
+    pair_send,
+    pair_recv,
+):
+    me = lax.axis_index("tp")
+    z, x, core = me // 4, lax.rem(me // 2, 2), lax.rem(me, 2)
+    across = z * 4 + (1 - x) * 2 + core
+    sibling = z * 4 + x * 2 + (1 - core)
+    wide, width = rows.shape[1], gate_w.shape[1]
+    tiles = gate_w.shape[0] // TILE
+    depth = rows_own.shape[0]
+    row_slots = arrived
+    cot_slots = cotangent
+
+    def block_at(slots, block):
+        return slots.at[pl.ds(pl.multiple_of(block * depth, depth), depth)]
+
+    def copy_to(which, block, send, target):
+        slots = row_slots if which == 0 else cot_slots
+        return pltpu.make_async_remote_copy(
+            src_ref=block_at(slots, block),
+            dst_ref=block_at(slots, block),
+            send_sem=send_sem.at[which, send],
+            recv_sem=recv_sem.at[which, block],
+            device_id={"tp": target},
+            device_id_type=MESH,
+        )
+
+    def weight_copy(tile, slot):
+        first = pl.ds(pl.multiple_of(lax.rem(tile, tiles) * TILE, TILE), TILE)
+        return first, weights.at[slot], weight_sem.at[slot]
+
+    def weight_start(tile, slot):
+        first, target, sem = weight_copy(tile, slot)
+
+        @pl.when(tile < tiles)
+        def _():
+            pltpu.make_async_copy(gate_w.at[first], target, sem).start()
+
+        @pl.when((tile >= tiles) & (tile < 2 * tiles))
+        def _():
+            pltpu.make_async_copy(up_w.at[first], target, sem).start()
+
+        @pl.when((tile >= 2 * tiles) & (tile < 3 * tiles))
+        def _():
+            pltpu.make_async_copy(down_w.at[first], target, sem).start()
+
+    def weight_wait(slot):
+        pltpu.make_async_copy(gate_w.at[pl.ds(0, TILE)], weights.at[slot], weight_sem.at[slot]).wait()
+
+    own_rows_copy = pltpu.make_async_copy(rows_own, block_at(row_slots, me), own_sem.at[0])
+    own_cot_copy = pltpu.make_async_copy(cotangent_own, block_at(cot_slots, me), own_sem.at[1])
+    own_rows_copy.start()
+    own_cot_copy.start()
+    weight_start(jnp.int32(0), 0)
+    weight_start(jnp.int32(1), 1)
+
+    barrier = pltpu.get_barrier_semaphore()
+    for step in range(1, 16):
+        pl.semaphore_signal(
+            barrier, inc=1, device_id={"tp": lax.rem(me + step, 16)}, device_id_type=MESH
+        )
+    pl.semaphore_wait(barrier, 15)
+
+    above, below = jnp.minimum(z + 1, 3), jnp.maximum(z - 1, 0)
+    above, below = above * 4 + x * 2 + core, below * 4 + x * 2 + core
+
+    def each_source(slot, side, act):
+        step = slot // 2 + 1
+        source = z - step if slot % 2 == 0 else z + step
+        valid = source >= 0 if slot % 2 == 0 else source <= 3
+        pl.when(valid)(lambda: act(source, source * 4 + (x if side == 0 else 1 - x) * 2 + core))
+
+    def send_own_column(which):
+        pl.when(z < 3)(lambda: copy_to(which, me, 0, above).start())
+        pl.when(z > 0)(lambda: copy_to(which, me, 4, below).start())
+
+    def send_across(which):
+        copy_to(which, me, 8 + z, across).start()
+
+    def send_sibling(which):
+        copy_to(which, me, 12 + z, sibling).start()
+
+    def column_event(which, slot):
+        def act(source, block):
+            copy_to(which, block, 0, sibling).wait_recv()
+            step = slot // 2 + 1
+            if slot % 2 == 0 and step < 3:
+                pl.when(z < 3)(lambda: copy_to(which, block, step, above).start())
+            if slot % 2 == 1 and step < 3:
+                pl.when(z > 0)(lambda: copy_to(which, block, 4 + step, below).start())
+            copy_to(which, block, 8 + source, across).start()
+            copy_to(which, block, 12 + source, sibling).start()
+
+        each_source(slot, 0, act)
+
+    def other_act(which):
+        def act(source, block):
+            copy_to(which, block, 0, sibling).wait_recv()
+            copy_to(which, block, 16 + source, sibling).start()
+
+        return act
+
+    def other_event(which, slot):
+        each_source(slot, 1, other_act(which))
+
+    def other_own(which):
+        other_act(which)(z, across)
+
+    own_rows_copy.wait()
+    own_cot_copy.wait()
+    send_own_column(0)
+    send_across(0)
+    send_sibling(0)
+    for slot in range(6):
+        column_event(0, slot)
+        if slot == 1:
+            other_own(0)
+        if slot == 3:
+            other_event(0, 0)
+            other_event(0, 1)
+    send_own_column(1)
+    send_across(1)
+    for slot in (2, 3, 4, 5):
+        other_event(0, slot)
+    send_sibling(1)
+
+    def last_wait(which):
+        for step in range(4):
+            for side in (0, 1):
+                block = lax.rem(z - step + 4, 4) * 4 + (x if side == 0 else 1 - x) * 2 + (1 - core)
+                copy_to(which, block, 0, sibling).wait_recv()
+
+    last_wait(0)
+
+    def panel_copy(index, slot):
+        columns = pl.ds(pl.multiple_of(index * PANEL, PANEL), PANEL)
+        return pltpu.make_async_copy(arrived.at[:, columns], panels.at[slot], panel_sem.at[slot])
+
+    count = wide // PANEL
+    panel_copy(0, 0).start()
+
+    @pl.loop(0, count)
+    def _(index):
+        slot = lax.rem(index, 2)
+
+        @pl.when(index + 1 < count)
+        def _():
+            panel_copy(index + 1, 1 - slot).start()
+
+        panel_copy(index, slot).wait()
+        columns = pl.ds(pl.multiple_of(index * PANEL, PANEL), PANEL)
+        rows[:, columns] = jnp.dot(
+            order[...], panels[slot], preferred_element_type=jnp.float32
+        ).astype(jnp.bfloat16)
+
+    def product(left, right, left_dim, right_dim):
+        return lax.dot_general(
+            left, right, (((left_dim,), (right_dim,)), ((), ())), preferred_element_type=jnp.float32
+        )
+
+    def project(left, slot, extra, out):
+        out[...] = product(left[:, width:], extra, 1, 1)
+
+        @pl.loop(0, width // CHUNK)
+        def _(part):
+            columns = pl.ds(pl.multiple_of(part * CHUNK, CHUNK), CHUNK)
+            out[...] += product(left[:, columns], weights[slot, :, columns], 1, 1)
+
+    @pl.loop(0, 2 * tiles)
+    def _(tile):
+        slot = lax.rem(tile, 2)
+
+        for at, events in (
+            (0, (lambda: column_event(1, 0), lambda: column_event(1, 1))),
+            (2, (lambda: column_event(1, 2), lambda: column_event(1, 3))),
+            (3, (lambda: other_own(1),)),
+            (5, (lambda: column_event(1, 4), lambda: column_event(1, 5))),
+            (7, (lambda: other_event(1, 0), lambda: other_event(1, 1))),
+            (10, (lambda: other_event(1, 2), lambda: other_event(1, 3))),
+        ):
+
+            @pl.when(tile == at)
+            def _(events=events):
+                for event in events:
+                    event()
+
+        weight_wait(slot)
+        own = pl.ds(pl.multiple_of(tile * TILE, TILE), TILE)
+        project(rows, slot, gate_ext[own, :], projected.at[tile])
+        weight_start(tile + 2, slot)
+
+    other_event(1, 4)
+    other_event(1, 5)
+    last_wait(1)
+    low_t = jnp.transpose(rows[:, width:].astype(jnp.float32)).astype(jnp.bfloat16)
+    grad_low_t = jnp.transpose(cotangent[:, width:].astype(jnp.float32)).astype(jnp.bfloat16)
+    partial[...] = jnp.zeros_like(partial)
+    share = pl.ds(pl.multiple_of(me * rows_mine.shape[1], rows_mine.shape[1]), rows_mine.shape[1])
+    rows_mine[...] = rows[:, share]
+    cotangent_mine[...] = cotangent[:, share]
+
+    @pl.loop(0, tiles)
+    def _(tile):
+        slot = lax.rem(tile, 2)
+        own = pl.ds(pl.multiple_of(tile * TILE, TILE), TILE)
+        weight_wait(slot)
+        project(cotangent, slot, down_ext[own, :], total)
+        weight_start(tile + 2 + 2 * tiles, slot)
+
+        @pl.loop(0, rows.shape[0] // STRIP)
+        def _(strip):
+            at = pl.ds(pl.multiple_of(strip * STRIP, STRIP), STRIP)
+            gate = projected[tile, at, :]
+            up = projected[tile + tiles, at, :]
+            grad = total[at, :]
+            sigmoid = 1.0 / (1.0 + jnp.exp(-gate))
+            active = gate * sigmoid
+            one = (active * up).astype(jnp.bfloat16)
+            two = (grad * up * sigmoid * (1.0 + gate * (1.0 - sigmoid))).astype(jnp.bfloat16)
+            three = (grad * active).astype(jnp.bfloat16)
+            hidden[at, :] = one
+            grad_gate[at, :] = two
+            grad_up[at, :] = three
+            partial[at, :] += (
+                product(one, hidden_back[own, :], 1, 0)
+                + product(two, gate_back[own, :], 1, 0)
+                + product(three, up_back[own, :], 1, 0)
+            )
+
+        gate_second[tile] = product(low_t, grad_gate[...], 1, 0)
+        up_second[tile] = product(low_t, grad_up[...], 1, 0)
+        down_first[tile] = product(grad_low_t, hidden[...], 1, 0)
+
+    def piece_copy(block, slot, target):
+        return pltpu.make_async_remote_copy(
+            src_ref=block_at(partial, block),
+            dst_ref=pieces.at[slot],
+            send_sem=pair_send.at[0, block],
+            recv_sem=pair_recv.at[0, slot],
+            device_id={"tp": target},
+            device_id_type=MESH,
+        )
+
+    def sum_copy(block, send, target):
+        return pltpu.make_async_remote_copy(
+            src_ref=block_at(summed, block),
+            dst_ref=block_at(summed, block),
+            send_sem=pair_send.at[1, send],
+            recv_sem=pair_recv.at[1, block],
+            device_id={"tp": target},
+            device_id_type=MESH,
+        )
+
+    @pl.loop(1, 16)
+    def _(step):
+        other = lax.rem(me + step, 16)
+        piece_copy(other, me, other).start()
+
+    pieces[me] = partial[pl.ds(pl.multiple_of(me * depth, depth), depth), :]
+
+    @pl.loop(1, 16)
+    def _(step):
+        piece_copy(me, lax.rem(me + step, 16), sibling).wait_recv()
+
+    summed[pl.ds(pl.multiple_of(me * depth, depth), depth), :] = jnp.sum(pieces[...], axis=0)
+
+    @pl.loop(1, 16)
+    def _(step):
+        other = lax.rem(me + step, 16)
+        sum_copy(me, other, other).start()
+
+    @pl.loop(1, 16)
+    def _(step):
+        sum_copy(lax.rem(me + step, 16), me, sibling).wait_recv()
+
+    summed_out[...] = summed[...]
+
+    @pl.loop(1, 16)
+    def _(step):
+        other = lax.rem(me + step, 16)
+        piece_copy(other, me, sibling).wait_send()
+        sum_copy(me, other, sibling).wait_send()
+
+    for which in (0, 1):
+        for step in range(3):
+            pl.when((z < 3) & (z >= step))(
+                lambda: copy_to(which, me, step, sibling).wait_send()
+            )
+            pl.when((z > 0) & (z + step <= 3))(
+                lambda: copy_to(which, me, 4 + step, sibling).wait_send()
+            )
+        for send in range(8, 20):
+            copy_to(which, me, send, sibling).wait_send()
+
+
+def layer(rows_own, cotangent_own, order, gate_w, up_w, down_w, gate_up_ext, down_ext, backs, mine):
+    depth, wide = rows_own.shape
+    tokens, units = order.shape[0], gate_w.shape[0]
+    tiles = units // TILE
+    bf16, f32 = jnp.bfloat16, jnp.float32
+    anywhere, vmem = pl.BlockSpec(memory_space=pl.ANY), pl.BlockSpec(memory_space=pltpu.VMEM)
+    return pl.pallas_call(
+        layer_kernel,
+        out_shape=(
+            jax.ShapeDtypeStruct((tokens, wide), bf16),
+            jax.ShapeDtypeStruct((tokens, 128), f32),
+            jax.ShapeDtypeStruct((tiles, 128, TILE), f32),
+            jax.ShapeDtypeStruct((tiles, 128, TILE), f32),
+            jax.ShapeDtypeStruct((tiles, 128, TILE), f32),
+            jax.ShapeDtypeStruct((tokens, mine), bf16),
+            jax.ShapeDtypeStruct((tokens, mine), bf16),
+        ),
+        in_specs=[anywhere, anywhere, vmem, anywhere, anywhere, anywhere] + [vmem] * 5,
+        out_specs=(anywhere,) + (vmem,) * 6,
+        scratch_shapes=[
+            pltpu.VMEM((tokens, wide), bf16),
+            pltpu.VMEM((tokens, wide), bf16),
+            pltpu.VMEM((2, TILE, wide - 128), bf16),
+            pltpu.VMEM((2 * tiles, tokens, TILE), f32),
+            pltpu.VMEM((2, tokens, PANEL), bf16),
+            pltpu.VMEM((tokens, TILE), f32),
+            pltpu.VMEM((tokens, TILE), bf16),
+            pltpu.VMEM((tokens, TILE), bf16),
+            pltpu.VMEM((tokens, TILE), bf16),
+            pltpu.SemaphoreType.DMA((2,)),
+            pltpu.SemaphoreType.DMA((2,)),
+            pltpu.SemaphoreType.DMA((2,)),
+            pltpu.SemaphoreType.DMA((2, 20)),
+            pltpu.SemaphoreType.DMA((2, 16)),
+            pltpu.VMEM((tokens, 128), f32),
+            pltpu.VMEM((16, depth, 128), f32),
+            pltpu.VMEM((tokens, 128), f32),
+            pltpu.SemaphoreType.DMA((2, 16)),
+            pltpu.SemaphoreType.DMA((2, 16)),
+        ],
+        compiler_params=pltpu.CompilerParams(
+            collective_id=0, has_side_effects=True, vmem_limit_bytes=62 * 1024 * 1024
+        ),
+    )(rows_own, cotangent_own, order, gate_w, up_w, down_w, gate_up_ext, down_ext, *backs)
+
+
+def at_columns(array, start):
+    return jnp.pad(array, ((0, 0), (start, 128 - start - array.shape[1])))
+
+
+def fused(normed_own, order, devices, my_index, width, rank, arrays):
+    gate_w, up_w, down_w, gate_first, gate_s, up_first, up_s, down_f, down_s, cot_own = arrays
+    both_first = jnp.concatenate([gate_first, up_first], axis=1)
+    low = narrow(normed_own, both_first, 1, 0).astype(jnp.bfloat16)
+    grad_low = narrow(cot_own, down_s, 1, 1).astype(jnp.bfloat16)
+    gate_t, up_t = gate_s.T, up_s.T
+    twice = jnp.bfloat16(ADAPTER_SCALE)
+    ext = jnp.concatenate(
+        [at_columns(twice * gate_t, 0), at_columns(twice * up_t, rank)], axis=0
+    )
+    _, total, gate_second, up_second, down_first, rows_mine, cot_mine = layer(
+        jnp.concatenate([normed_own, at_columns(low, 0)], axis=1),
+        jnp.concatenate([cot_own, at_columns(grad_low, 0)], axis=1),
+        order,
+        gate_w,
+        up_w,
+        down_w,
+        ext,
+        at_columns(twice * down_f, 0),
+        (at_columns(down_f, 0), at_columns(gate_t, rank), at_columns(up_t, 2 * rank)),
+        width // devices,
+    )
+
+    def second(tiled, start):
+        cut = ADAPTER_SCALE * tiled[:, start : start + rank, :]
+        return cut.transpose(1, 0, 2).reshape(rank, -1)
+
+    both = ADAPTER_SCALE * exact(rows_mine, total[:, rank : 3 * rank], 0, 0)
+    down_second = ADAPTER_SCALE * exact(total[:, :rank], cot_mine, 0, 0)
+    return (
+        both[:, :rank],
+        second(gate_second, 0),
+        both[:, rank:],
+        second(up_second, rank),
+        second(down_first, 0).T,
+        down_second,
+    )
 
 
 def shards(
@@ -76,6 +505,27 @@
         devices,
         my_index,
     )
+    if devices == 16 and normed_own.shape[0] == output_cotangent_rows.shape[0] == 48:
+        return fused(
+            normed_own,
+            order,
+            devices,
+            my_index,
+            width,
+            rank,
+            (
+                gate_projection_matrix,
+                up_projection_matrix,
+                down_projection_matrix,
+                gate_adapter_first,
+                gate_adapter_second,
+                up_adapter_first,
+                up_adapter_second,
+                down_adapter_first,
+                down_adapter_second,
+                output_cotangent_rows,
+            ),
+        )
     arrived = lax.all_gather(normed_own, "tp", axis=0, tiled=True)
     cotangent = lax.all_gather(output_cotangent_rows, "tp", axis=0, tiled=True)
     normed = narrow(order, arrived, 1, 0).astype(jnp.bfloat16)

time: 366 us -> 288 us (0.79)
  Pallas kernels: 0 us -> 260 us
  waiting for transfers between devices: 207 us -> 0 us
  matrix products: 137 us -> 6.54 us
  between operations: 13.9 us -> 0.84 us
  local copies, waits for them, and re-layouts: 1.63 us -> 8.98 us
  other arithmetic: 5.77 us -> 9.85 us
    pallas_call x0 -> x1, Pallas kernels: none -> 260 us  [layer(): pl.pallas_call(layer_kernel, out_shape=(jax.ShapeDtypeStruct((tokens, wid...]
    dot_general x16 -> x3, matrix products: 133 us -> 2.2 us  [narrow(): lax.dot_general(left, right, (((left_dim,), (right_dim,)), ((), ())), pre...]
    all_gather x2 -> x0, waiting for transfers between devices: 123 us -> none  [the longest x1 102 us: shards(): arrived = lax.all_gather(normed_own, 'tp', axis=0, tiled=True)]
    psum x1 -> x0, waiting for transfers between devices: 83.2 us -> none  [shards(): total = lax.psum(partial, 'tp')]
    pad x0 -> x4, local copies, waits for them, and re-layouts: none -> 3.72 us  [at_columns(): return jnp.pad(array, ((0, 0), (start, 128 - start - array.shape[1])))]
  transfers between devices with their start and end apart: 3 -> 0, of which waited for: 3 -> 0; matrix products, arithmetic and copies ran while one was open for 23% -> 0% of each run, Pallas kernels for 0% -> 0%
where the time goes in v2:
time: 288 us; the launch traced here: 287 us
  Pallas kernels  260 us (90%)
  other arithmetic  9.85 us (3%)
  local copies, waits for them, and re-layouts  8.98 us (3%)
  matrix products  6.54 us (2%)
    pallas_call x1, Pallas kernels, layer(): pl.pallas_call(layer_kernel, out_shape=(jax.ShapeDtypeStruct((tokens, wid...  260 us

profile of v2, /device:TPU:0, one launch (start us, length us, event | category | flops | bytes accessed | tf_op | source)
XLA Modules:
  0.0 286.7 jit_solution(8143759155723547977)
XLA Ops:
  0.7 0.8 and_select_fusion
  1.5 0.7 broadcast_compare_fusion
  2.1 0.2 convert_reduce_fusion
  2.3 0.1 select_reduce_fusion
  2.6 1.5 convolution_convert_fusion.1
  4.4 0.7 convert_element_type.39
  5.2 0.1 add.110
  5.3 1.1 copy.46
  6.4 0.3 copy.47
  6.7 0.3 copy.48
  7.0 0.9 pad.34.hidden_back
  7.9 0.9 pad.33.down_ext
  8.7 1.0 pad.36.up_back
  9.8 1.0 pad.35.gate_back
  10.8 1.2 fusion.5.gate_ext
  12.0 0.3 fusion.14
  12.4 0.2 multiply_reduce_fusion
  12.6 0.2 multiply_convert_fusion
  12.9 0.5 copy-done.6
  13.4 0.4 convolution_convert_fusion
  13.9 1.3 fusion.6
  15.2 1.4 fusion.order
  16.5 260.4 %shard_map.181 = (bf16[768,8320]{1,0:T(8,128)(2,1)}, f32[768,128]{1,0:T(8,128)}, f32[7,128,256]{2,1,0:T(8,128)}, f32[7,128,256]{2,1,0:T(8,128)}, f32[7,128,256]{...) custom-call(bf16[48,8320]{1,0:T(8,128)(2,1)} %get-tuple-element.24.rows_own, ...), custom_call_target="tpu_custom_call" | custom-call | tf_op jit(solution)/shard_map/pallas_call | solution.py:397
  277.0 2.0 convolution_multiply_fusion
  279.0 2.3 convolution_multiply_fusion.1
  281.3 0.6 fusion.18
  282.0 0.9 multiply_bitcast_fusion.2
  282.9 0.7 copy.53
  283.5 0.9 multiply_bitcast_fusion.1
  284.4 0.7 copy.54
  285.1 0.9 multiply_bitcast_fusion
  286.0 0.7 copy.55
  (30 shorter events, 0.9 us)
Async XLA Ops:
  0.6 11.4 %copy-start = (bf16[64,8192]{1,0:T(8,128)(2,1)S(1)}, bf16[64,8192]{1,0:T(8,128)(2,1)}, u32[]{:S(2)}) copy-start(bf16[64,8192]{1,0:T(8,128)(2,1)} %param.14) | copy-start | bytes 3145732
  0.6 6.0 %copy-start.5 = (bf16[1792,16]{0,1:T(8,128)(2,1)S(1)}, bf16[1792,16]{0,1:T(8,128)(2,1)}, u32[]{:S(2)}) copy-start(bf16[1792,16]{0,1:T(8,128)(2,1)} %param.25) | copy-start | bytes 172036
  0.7 5.7 %copy-start.4 = (bf16[16,1792]{1,0:T(8,128)(2,1)S(1)}, bf16[16,1792]{1,0:T(8,128)(2,1)}, u32[]{:S(2)}) copy-start(bf16[16,1792]{1,0:T(8,128)(2,1)} %param.24) | copy-start | bytes 172036
  7.9 2.9 copy-start.3
  12.4 1.0 copy-start.6
  12.4 1.0 copy-start.7
  12.6 1.2 copy-start.2
  277.0 9.7 %copy-start.1 = (bf16[64,8192]{1,0:T(8,128)(2,1)S(1)}, bf16[64,8192]{1,0:T(8,128)(2,1)}, u32[]{:S(2)}) copy-start(bf16[64,8192]{1,0:T(8,128)(2,1)} %param.14) | copy-start | bytes 3145732
